TPU v7x, 32 devices: a whole 2x2x4 slice. The times are simulated.
32 devices in a mesh: slab: 4 (over z), member: 8 (over y, x, core).
Axes of the slice: x: 2, y: 2, z: 4, core: 2. Of those that a mesh axis runs over, the one named last changes fastest.
Arguments:
- state: float32 [16, 64, 4096], P('member', 'slab'), may hold values from -6 to 6
- winds: float32 [2, 64, 4096], P(None, 'slab'), may hold values from -0.35 to 0.35
- kappa: float32 [64, 4096], P('slab'), may hold values from 0.05 to 0.22
- obs_values: float32 [512, 128], P('slab'), may hold values from -6 to 6
- obs_rinv: float32 [512, 128], P('slab'), may hold values from 0.1 to 1
- owner: int32 [512, 1], P('slab'), may hold values from 0 to 3; in each aligned block of 128 rows (0 to 127, 128 to 255, ...) at most 64 rows name the same one
- obs_rows: int32 [512], P('slab'), may hold values from 0 to 15
- obs_tiles: int32 [512], P('slab'), may hold values from 0 to 31
- counts: int32 [4], P('slab'), may hold values from 64 to 128, as said below
- tile_mask: int32 [4, 32, 32], P('slab'), may hold values 0 or 1
Outputs:
- analysis: float32 [16, 64, 4096], P('member', 'slab')
Inputs may be any that keep to these rules, and one draw needn't show every extreme that they name: Among the 128 profile rows of one slab index at most 64 name the same owner, a bound that some block reaches of them. `counts`: some slab index has all 128 rows live.
All inputs are finite; a program needn't handle non-finite values. No bound on the sum of `tile_mask` on one device may be relied on, other than what follows from the above.
Results may differ from a plain program's by a relative error of at most 0.00011.
Values sent between devices are 32-bit elements; how exact they have to be, the bound alone decides.
A program may use at most 64 MiB of HBM per device.

v0:
```python
import math
import jax
import jax.numpy as jnp
from jax import lax
from jax.sharding import PartitionSpec as P

PROF = 128
FSTEPS = 2
NS_ITERS = 6
HIGHEST_PRECISION = lax.Precision.HIGHEST


def padded(cells, sides, width):
    for axis, dim in sides:
        count = lax.axis_size(axis)
        ends = count - 1
        head = lax.slice_in_dim(cells, 0, width, axis=dim)
        tail = lax.slice_in_dim(cells, cells.shape[dim] - width, cells.shape[dim], axis=dim)
        cells = jnp.concatenate(
            [
                lax.ppermute(tail, axis, [(i, (i + 1) % count) for i in range(ends)]),
                cells,
                lax.ppermute(head, axis, [((i + 1) % count, i) for i in range(ends)]),
            ],
            axis=dim,
        )
    return cells


def step_forward_border(widened_field, coeff_east, coeff_north, diffusion):
    middle_row = widened_field[:, 1:-1]
    northern_row = widened_field[:, 2:]
    southern_row = widened_field[:, :-2]
    eastern_column = jnp.roll(middle_row, -1, 2)
    western_column = jnp.roll(middle_row, 1, 2)
    return (
        middle_row
        - coeff_east * (eastern_column - western_column) * 0.5
        - coeff_north * (northern_row - southern_row) * 0.5
        + diffusion
        * (eastern_column + western_column + northern_row + southern_row - 4.0 * middle_row)
    )


def inverse_root(matrix, order_size):
    identity = jnp.eye(order_size, dtype=jnp.float32)
    frob_norm = jnp.sqrt(jnp.sum(matrix * matrix, axis=(-2, -1), keepdims=True) + 1e-06)
    iterate = matrix / frob_norm
    factor = jnp.broadcast_to(identity, matrix.shape)
    for step_number in range(NS_ITERS):
        middle = 1.5 * identity - 0.5 * jnp.matmul(factor, iterate, precision=HIGHEST_PRECISION)
        iterate = jnp.matmul(iterate, middle, precision=HIGHEST_PRECISION)
        factor = jnp.matmul(middle, factor, precision=HIGHEST_PRECISION)
    return factor / jnp.sqrt(frob_norm)


def weights_for(gram_total, innov_total, members):
    identity = jnp.eye(members, dtype=jnp.float32)
    inv_root = inverse_root(gram_total + (members - 1.0) * identity, members)
    half_step = jnp.einsum("...ij,...j->...i", inv_root, innov_total, precision=HIGHEST_PRECISION)
    mean_shift = jnp.einsum("...ij,...j->...i", inv_root, half_step, precision=HIGHEST_PRECISION)
    return mean_shift[..., :, None] + math.sqrt(members - 1.0) * inv_root


def on_device(
    state, winds, kappa, obs_values, obs_rinv, owner, obs_rows, obs_tiles, counts, tile_mask
):
    lat_rows = state.shape[1]
    predict_members = state
    for step_number in range(FSTEPS):
        widened_field = padded(predict_members, (("slab", 1),), 1)
        predict_members = step_forward_border(widened_field, winds[0], winds[1], kappa)
    cell_major_layout = lax.all_to_all(
        predict_members, "member", split_axis=2, concat_axis=0, tiled=True
    )
    ensemble = cell_major_layout.shape[0]
    cell_width = cell_major_layout.shape[2]
    tiles_here = cell_width // PROF
    ensemble_average = jnp.mean(cell_major_layout, axis=0)
    member_deviation = cell_major_layout - ensemble_average
    slab_count = lax.axis_size("slab")
    per_slab = owner.shape[0]
    first_tile = lax.axis_index("member") * tiles_here
    cells = lat_rows * tiles_here
    tile_off = obs_tiles - first_tile
    inside = (
        (tile_off >= 0)
        & (tile_off < tiles_here)
        & (jnp.arange(per_slab, dtype=jnp.int32) < counts[0])
    )
    target = jnp.where(inside, owner[:, 0] * cells + obs_rows * tiles_here + tile_off, -1)
    placing = (target[None, :] == jnp.arange(slab_count * cells, dtype=jnp.int32)[:, None]).astype(
        jnp.float32
    )
    payload = jnp.concatenate([obs_rinv, obs_rinv * obs_values], axis=1)
    sums = jnp.matmul(placing, payload, precision=HIGHEST_PRECISION)
    sums = lax.all_to_all(
        sums.reshape(slab_count, lat_rows, tiles_here, 2, PROF),
        "slab",
        split_axis=0,
        concat_axis=0,
        tiled=True,
    )
    sums = jnp.sum(sums, axis=0)
    cell_weight, cell_value = (sums[:, :, 0], sums[:, :, 1])
    blocks = member_deviation.reshape(ensemble, lat_rows, tiles_here, PROF)
    mean_blocks = ensemble_average.reshape(lat_rows, tiles_here, PROF)
    gram_here = jnp.einsum(
        "irth,jrth->tij", blocks * cell_weight, blocks, precision=HIGHEST_PRECISION
    )
    innov_here = jnp.einsum(
        "irth,rth->ti", blocks, cell_value - cell_weight * mean_blocks, precision=HIGHEST_PRECISION
    )
    tile_count = tile_mask.shape[1]
    tile_use = jnp.maximum(tile_mask[0].astype(jnp.float32), jnp.eye(tile_count, dtype=jnp.float32))
    use_mine = lax.dynamic_slice_in_dim(tile_use, first_tile, tiles_here, 0)
    gram_next = jnp.einsum(
        "ts,sij->tij",
        use_mine,
        lax.all_gather(gram_here, "member", axis=0, tiled=True),
        precision=HIGHEST_PRECISION,
    )
    innov_next = jnp.einsum(
        "ts,si->ti",
        use_mine,
        lax.all_gather(innov_here, "member", axis=0, tiled=True),
        precision=HIGHEST_PRECISION,
    )
    mixing = weights_for(gram_next, innov_next, ensemble)
    update = jnp.einsum("irth,tij->jrth", blocks, mixing, precision=HIGHEST_PRECISION)
    update = update + ensemble_average.reshape(lat_rows, tiles_here, PROF)
    return lax.all_to_all(
        update.reshape(ensemble, lat_rows, cell_width),
        "member",
        split_axis=0,
        concat_axis=2,
        tiled=True,
    )


def solution(mesh):
    placed = (
        P("member", "slab", None),
        P(None, "slab", None),
        P("slab", None),
        P("slab", None),
        P("slab", None),
        P("slab", None),
        P("slab"),
        P("slab"),
        P("slab"),
        P("slab", None, None),
    )
    return jax.shard_map(
        on_device, mesh=mesh, in_specs=placed, out_specs=P("member", "slab", None), check_vma=False
    )
```

profile of v0, /device:TPU:0, one launch (start us, length us, event | category | flops | bytes accessed | tf_op | source)
XLA Modules:
  0.0 106.8 jit_solution(4325995497282656139)
XLA Ops:
  0.0 1.2 %fusion.48 = (f32[2,1,4096]{2,1,0:T(1,128)S(1)}, f32[2,1,4096]{2,1,0:T(1,128)S(1)}) fusion(f32[2,16,4096]{2,1,0:T(8,128)} %param.10), kind=kLoop, calls=%fused_computation.86 | loop fusion | bytes 131072 | tf_op jit(solution)/shard_map/slice | solution.py:18
  1.2 1.3 %collective-permute-start = (f32[2,1,4096]{2,0,1:T(2,128)S(1)}, f32[2,1,4096]{2,0,1:T(2,128)S(1)}, u32[]{:S(2)}, u32[]{:S(2)}) collective-permute-start(f32[2,1,4096]{2,0,1:T(2,128)S(1)} %copy.153), channel_id=1, source_target_pairs={{8,0},{16,8},{24,16},{9,1},{17,9},{25,17},{10,2},{18,10},{26,18},{... | collective-permute-start | bytes 98312 | tf_op jit(solution)/shard_map/ppermute | solution.py:23
  2.6 5.6 %collective-permute-start.1 = (f32[2,1,4096]{2,0,1:T(2,128)S(1)}, f32[2,1,4096]{2,0,1:T(2,128)S(1)}, u32[]{:S(2)}, u32[]{:S(2)}) collective-permute-start(f32[2,1,4096]{2,0,1:T(2,128)S(1)} %copy.154), channel_id=1, source_target_pairs={{0,8},{8,16},{16,24},{1,9},{9,17},{17,25},{2,10},{10,18},{18,26},{... | collective-permute-start | bytes 98312 | tf_op jit(solution)/shard_map/ppermute | solution.py:21
  8.8 0.9 mul.169
  9.7 0.7 and_select_fusion
  10.4 1.1 %fusion.14 = f32[256,256]{1,0:T(8,128)S(1)} fusion(f32[128,128]{1,0:T(8,128)S(1)} %mul.169, f32[128,128]{1,0:T(8,128)} %param.14, s32[128]{0:T(128)S(1)} %and_select_fusion), kind=kOutput, calls=%fused_computation.38 | convolution fusion | flops 100728832 | bytes 393728 | tf_op jit(solution)/shard_map/dot_general | solution.py:96
  11.5 0.8 reshape.53
  12.3 4.3 %all-to-all-start.1 = ((f32[4,16,4,2,128]{4,3,2,1,0:T(2,128)}), f32[4,16,4,2,128]{4,3,2,1,0:T(2,128)S(1)}, u32[]{:S(2)}, u32[]{:S(2)}) async-start(f32[4,16,4,2,128]{4,3,2,1,0:T(2,128)} %reshape.53), calls=%async_computation.1 | async-start | bytes 524288 | tf_op jit(solution)/shard_map/all_to_all | solution.py:97
  16.6 1.5 %fusion.46 = (f32[2,16,4095]{2,1,0:T(8,128)S(1)}, f32[2,16,4095]{2,1,0:T(8,128)S(1)}) fusion(f32[2,16,4096]{2,1,0:T(8,128)} %param.10), kind=kLoop, calls=%fused_computation.84 | loop fusion | bytes 2096640 | tf_op jit(solution)/shard_map/jit(_roll_static)/slice | solution.py:34
  18.1 0.8 fusion.47
  19.0 0.0 collective-permute-done
  19.0 0.0 collective-permute-done.1
  19.1 0.5 multiply_add_fusion.1
  19.6 0.2 fusion.43
  19.9 1.3 %collective-permute-start.2 = (f32[2,1,4096]{2,0,1:T(2,128)S(1)}, f32[2,1,4096]{2,0,1:T(2,128)S(1)}, u32[]{:S(2)}, u32[]{:S(2)}) collective-permute-start(f32[2,1,4096]{2,0,1:T(2,128)S(1)} %copy.127), channel_id=1, source_target_pairs={{8,0},{16,8},{24,16},{9,1},{17,9},{25,17},{10,2},{18,10},{26,18},{... | collective-permute-start | bytes 98312 | tf_op jit(solution)/shard_map/ppermute | solution.py:23
  21.2 4.6 %collective-permute-start.3 = (f32[2,1,4096]{2,0,1:T(2,128)S(1)}, f32[2,1,4096]{2,0,1:T(2,128)S(1)}, u32[]{:S(2)}, u32[]{:S(2)}) collective-permute-start(f32[2,1,4096]{2,0,1:T(2,128)S(1)} %copy.129), channel_id=1, source_target_pairs={{0,8},{8,16},{16,24},{1,9},{9,17},{17,25},{2,10},{10,18},{18,26},{... | collective-permute-start | bytes 98312 | tf_op jit(solution)/shard_map/ppermute | solution.py:21
  25.8 0.1 fusion.44
  25.8 0.0 collective-permute-done.2
  25.9 1.5 %collective-permute-done.3 = f32[2,1,4096]{2,0,1:T(2,128)S(1)} collective-permute-done((f32[2,1,4096]{2,0,1:T(2,128)S(1)}, f32[2,1,4096]{2,0,1:T(2,128)S(1)}, u32[]{:S(2)}, u32[]{:S(2)}) %collective-permute-start.3) | collective-permute-done | bytes 32800 | tf_op jit(solution)/shard_map/ppermute | solution.py:21
  27.4 0.5 multiply_add_fusion
  27.8 0.0 copy-start.3
  27.9 4.3 %copy.131 = f32[2,16,4096]{1,0,2:T(2,128)} copy(f32[2,16,4096]{2,1,0:T(8,128)S(1)} %multiply_add_fusion) | data formatting | bytes 1048576 | tf_op jit(solution)/shard_map/add | solution.py:37
  32.2 7.9 %reshape.66 = f32[8,1,16384]{2,1,0:T(1,128)} reshape(f32[4096,2,16]{2,1,0:T(2,128)} %bitcast.106) | data formatting | bytes 1048576
  40.1 0.0 all-to-all-done.1
  40.1 3.7 %all-to-all-start = ((f32[8,1,16384]{2,1,0:T(1,128)}), f32[8,1,16384]{2,1,0:T(1,128)S(1)}, u32[]{:S(2)}, u32[]{:S(2)}) async-start(f32[8,1,16384]{2,1,0:T(1,128)} %reshape.66), calls=%async_computation | async-start | bytes 1048576 | tf_op jit(solution)/shard_map/all_to_all | solution.py:73
  43.8 0.1 reduce_sum.28
  44.0 0.1 fusion.49
  44.0 9.5 %all-to-all-done = f32[8,1,16384]{2,1,0:T(1,128)S(1)} async-done(((f32[8,1,16384]{2,1,0:T(1,128)}), f32[8,1,16384]{2,1,0:T(1,128)S(1)}, u32[]{:S(2)}, u32[]{:S(2)}) %all-to-all-start) | async-done | bytes 524320 | tf_op jit(solution)/shard_map/all_to_all | solution.py:73
  53.5 0.5 broadcast.96
  54.1 1.9 %reduce.1 = f32[8,16384]{1,0:T(8,128)S(1)} reduce(f32[8,1,16384]{2,1,0:T(1,128)S(1)} %all-to-all-done, f32[]{:T(128)} %broadcast.96), dimensions={1}, to_apply=%all_to_all.29.reduce_sub_computation | reduce | bytes 1048580 | tf_op jit(solution)/shard_map/all_to_all | solution.py:73
  56.0 7.5 %reshape.67 = f32[4096,2,16]{2,1,0:T(2,128)} reshape(f32[8,16384]{1,0:T(8,128)S(1)} %reduce.1) | data formatting | bytes 1048576
  63.5 5.1 %copy.132 = f32[2,16,8,512]{3,1,0,2:T(8,128)S(1)} copy(f32[2,16,8,512]{1,0,3,2:T(2,128)} %bitcast.107) | data formatting | bytes 1048576 | tf_op jit(solution)/shard_map/all_to_all | solution.py:73
  68.7 0.2 all_to_all.32
  68.9 1.1 %convolution_bitcast_fusion.1 = f32[4,16,16]{2,1,0:T(8,128)S(1)} fusion(f32[16,16,4,128]{3,2,1,0:T(4,128)S(1)} %all_to_all.32, f32[16,4,128]{2,0,1:T(8,128)S(1)} %copy.136, f32[16,4,128]{2,0,1:T(8,128)S(1)} %bitcast.110), kind=kOutput, calls=%fused_computation.16 | convolution fusion | flops 25559040 | bytes 593920 | tf_op jit(solution)/shard_map/irth,jrth->tij/dot_general | solution.py:108
  70.0 8.4 %all_gather.6 = f32[32,16,16]{2,1,0:T(8,128)S(1)} all-gather(f32[4,16,16]{2,1,0:T(8,128)S(1)} %convolution_bitcast_fusion.1), channel_id=1, replica_groups=mesh['slab'=4,'member'=8] {'member'}, dimensions={0}, use_global_device_ids=true | all-gather | bytes 36864 | tf_op jit(solution)/shard_map/all_gather | solution.py:120
  78.4 0.4 multiply_reduce_fusion
  78.8 0.1 broadcast_divide_fusion
  78.9 0.2 fusion.6
  79.1 0.2 fusion.23
  79.2 0.2 fusion.28
  79.4 0.2 fusion.5
  79.6 0.2 fusion.51
  79.7 0.2 fusion.50
  79.9 0.2 fusion.4
  80.1 0.2 fusion.53
  80.3 0.2 fusion.52
  80.4 0.2 fusion.3
  80.6 0.2 fusion.55
  80.8 0.2 fusion.54
  80.9 0.2 fusion.2
  81.1 0.2 fusion.57
  81.3 0.2 fusion.56
  81.5 1.0 fusion.8
  82.5 8.9 %all-gather = f32[8,4,16]{2,1,0:T(4,128)S(1)} all-gather(f32[1,4,16]{2,1,0:T(4,128)S(1)} %bitcast.118), channel_id=1, replica_groups=mesh['slab'=4,'member'=8] {'member'}, dimensions={0}, use_global_device_ids=true | all-gather | bytes 2304 | tf_op jit(solution)/shard_map/all_gather | solution.py:126
  91.4 0.1 fusion.35
  91.5 0.2 fusion.1
  91.7 0.2 convolution_divide_fusion
  91.9 0.2 convolution_bitcast_fusion.2
  92.0 0.2 fusion.58
  92.2 0.9 fusion
  93.2 0.3 copy.141
  93.5 0.2 reshape.54
  93.7 12.3 %all_to_all.41 = f32[16,16,512]{2,1,0:T(8,128)S(1)} all-to-all(f32[16,16,512]{2,1,0:T(8,128)S(1)} %reshape.54), channel_id=1, replica_groups=mesh['slab'=4,'member'=8] {'member'}, dimensions={0} | all-to-all | bytes 1048576 | tf_op jit(solution)/shard_map/all_to_all | solution.py:132
  106.0 0.8 copy.157
  (28 shorter events, 0.5 us)
Async XLA Ops:
  0.0 19.1 %copy-start = (f32[2,16,4096]{2,1,0:T(8,128)S(1)}, f32[2,16,4096]{2,1,0:T(8,128)}, u32[]{:S(2)}) copy-start(f32[2,16,4096]{2,1,0:T(8,128)} %param.10) | copy-start | bytes 1572868
  0.0 18.9 %copy-start.2 = (f32[2,16,4096]{2,1,0:T(8,128)S(1)}, f32[2,16,4096]{2,1,0:T(8,128)}, u32[]{:S(2)}) copy-start(f32[2,16,4096]{2,1,0:T(8,128)} %param.11) | copy-start | bytes 1572868
  0.0 19.1 %copy-start.1 = (f32[16,4096]{1,0:T(8,128)S(1)}, f32[16,4096]{1,0:T(8,128)}, u32[]{:S(2)}) copy-start(f32[16,4096]{1,0:T(8,128)} %param.12) | copy-start | bytes 786436
  1.2 17.8 %collective-permute-start = (f32[2,1,4096]{2,0,1:T(2,128)S(1)}, f32[2,1,4096]{2,0,1:T(2,128)S(1)}, u32[]{:S(2)}, u32[]{:S(2)}) collective-permute-start(f32[2,1,4096]{2,0,1:T(2,128)S(1)} %copy.153), channel_id=1, source_target_pairs={{8,0},{16,8},{24,16},{9,1},{17,9},{25,17},{10,2},{18,10},{26,18},{... | collective-permute-start | bytes 98312 | tf_op jit(solution)/shard_map/ppermute | solution.py:23
  2.6 16.5 %collective-permute-start.1 = (f32[2,1,4096]{2,0,1:T(2,128)S(1)}, f32[2,1,4096]{2,0,1:T(2,128)S(1)}, u32[]{:S(2)}, u32[]{:S(2)}) collective-permute-start(f32[2,1,4096]{2,0,1:T(2,128)S(1)} %copy.154), channel_id=1, source_target_pairs={{0,8},{8,16},{16,24},{1,9},{9,17},{17,25},{2,10},{10,18},{18,26},{... | collective-permute-start | bytes 98312 | tf_op jit(solution)/shard_map/ppermute | solution.py:21
  12.3 27.8 %all-to-all-start.1 = ((f32[4,16,4,2,128]{4,3,2,1,0:T(2,128)}), f32[4,16,4,2,128]{4,3,2,1,0:T(2,128)S(1)}, u32[]{:S(2)}, u32[]{:S(2)}) async-start(f32[4,16,4,2,128]{4,3,2,1,0:T(2,128)} %reshape.53), calls=%async_computation.1 | async-start | bytes 524288 | tf_op jit(solution)/shard_map/all_to_all | solution.py:97
  19.9 6.0 %collective-permute-start.2 = (f32[2,1,4096]{2,0,1:T(2,128)S(1)}, f32[2,1,4096]{2,0,1:T(2,128)S(1)}, u32[]{:S(2)}, u32[]{:S(2)}) collective-permute-start(f32[2,1,4096]{2,0,1:T(2,128)S(1)} %copy.127), channel_id=1, source_target_pairs={{8,0},{16,8},{24,16},{9,1},{17,9},{25,17},{10,2},{18,10},{26,18},{... | collective-permute-start | bytes 98312 | tf_op jit(solution)/shard_map/ppermute | solution.py:23
  21.2 6.1 %collective-permute-start.3 = (f32[2,1,4096]{2,0,1:T(2,128)S(1)}, f32[2,1,4096]{2,0,1:T(2,128)S(1)}, u32[]{:S(2)}, u32[]{:S(2)}) collective-permute-start(f32[2,1,4096]{2,0,1:T(2,128)S(1)} %copy.129), channel_id=1, source_target_pairs={{0,8},{8,16},{16,24},{1,9},{9,17},{17,25},{2,10},{10,18},{18,26},{... | collective-permute-start | bytes 98312 | tf_op jit(solution)/shard_map/ppermute | solution.py:21
  27.8 16.0 %copy-start.3 = (s32[1,32,32]{2,1,0:T(8,128)S(1)}, s32[1,32,32]{2,1,0:T(8,128)}, u32[]{:S(2)}) copy-start(s32[1,32,32]{2,1,0:T(8,128)} %param.19) | copy-start | bytes 12292
  40.1 13.5 %all-to-all-start = ((f32[8,1,16384]{2,1,0:T(1,128)}), f32[8,1,16384]{2,1,0:T(1,128)S(1)}, u32[]{:S(2)}, u32[]{:S(2)}) async-start(f32[8,1,16384]{2,1,0:T(1,128)} %reshape.66), calls=%async_computation | async-start | bytes 1048576 | tf_op jit(solution)/shard_map/all_to_all | solution.py:73
where the time goes:
time: 108 us; the launch traced here: 107 us
  local copies, waits for them, and re-layouts  32 us (30%)
  blocking collectives  29.5 us (27%)
  starting transfers between devices  20.7 us (19%)
  waiting for transfers between devices  11 us (10%)
  matrix products  7.89 us (7%)
  other arithmetic  4.66 us (4%)
  between operations  1.08 us (1%)
    unnamed x12, local copies, waits for them, and re-layouts  15.5 us
    all_to_all x1, blocking collectives, on_device(): lax.all_to_all(update.reshape(ensemble, lat_rows, cell_width), 'member',...  12.3 us
    ppermute x2, starting transfers between devices, padded(): lax.ppermute(tail, axis, [(i, (i + 1) % count) for i in range(ends)])  10.1 us
    all_to_all x1, waiting for transfers between devices, on_device(): lax.all_to_all(predict_members, 'member', split_axis=2, concat_axis=0, ti...  9.52 us
    all_gather x1, blocking collectives, on_device(): lax.all_gather(innov_here, 'member', axis=0, tiled=True)  8.86 us
    all_gather x1, blocking collectives, on_device(): lax.all_gather(gram_here, 'member', axis=0, tiled=True)  8.35 us
    all_to_all x3, local copies, waits for them, and re-layouts, on_device(): lax.all_to_all(predict_members, 'member', split_axis=2, concat_axis=0, ti...  5.82 us
    add x1, local copies, waits for them, and re-layouts, step_forward_border(): middle_row - coeff_east * (eastern_column - western_column) * 0.5  4.34 us
  transfers between devices with their start and end apart: 6, of which 2 were waited for; matrix products, arithmetic and copies ran while one was open for 18% of the time, Pallas kernels for 0%

commit v1 on v0

--- a/solution.py
+++ b/solution.py
@@ -70,8 +70,14 @@
     for step_number in range(FSTEPS):
         widened_field = padded(predict_members, (("slab", 1),), 1)
         predict_members = step_forward_border(widened_field, winds[0], winds[1], kappa)
-    cell_major_layout = lax.all_to_all(
-        predict_members, "member", split_axis=2, concat_axis=0, tiled=True
+    cell_major_layout = jnp.concatenate(
+        lax.all_to_all(
+            jnp.stack(jnp.split(predict_members, lax.axis_size("member"), axis=2)),
+            split_axis=0,
+            axis_name="member",
+            concat_axis=0,
+        ),
+        axis=0,
     )
     ensemble = cell_major_layout.shape[0]
     cell_width = cell_major_layout.shape[2]

time: 108 us -> 82.8 us (0.77)
  local copies, waits for them, and re-layouts: 32 us -> 11.6 us
  other arithmetic: 4.66 us -> 1.18 us
    unnamed x12 -> x25, local copies, waits for them, and re-layouts: 15.5 us -> 6.76 us
    all_to_all x3 -> x0, local copies, waits for them, and re-layouts: 5.82 us -> none  [on_device(): lax.all_to_all(predict_members, 'member', split_axis=2, concat_axis=0, ti...]
    add x1 -> x0, local copies, waits for them, and re-layouts: 4.34 us -> none  [step_forward_border(): middle_row - coeff_east * (eastern_column - western_column) * 0.5]
    slice x4, local copies, waits for them, and re-layouts: 2.59 us -> 0.55 us  [step_forward_border(): eastern_column = jnp.roll(middle_row, -1, 2)]
    all_to_all x1 -> x0, other arithmetic: 1.88 us -> none  [on_device(): lax.all_to_all(predict_members, 'member', split_axis=2, concat_axis=0, ti...]
  transfers between devices with their start and end apart: 6 -> 6, of which waited for: 2 -> 3; matrix products, arithmetic and copies ran while one was open for 18% -> 10% of each run, Pallas kernels for 0% -> 0%
where the time goes in v1:
time: 82.8 us; the launch traced here: 82.2 us
  blocking collectives  29.5 us (36%)
  starting transfers between devices  20.8 us (25%)
  local copies, waits for them, and re-layouts  11.6 us (14%)
  waiting for transfers between devices  11 us (13%)
  matrix products  7.04 us (9%)
  other arithmetic  1.18 us (1%)
  between operations  1.04 us (1%)
    all_to_all x1, blocking collectives, on_device(): lax.all_to_all(update.reshape(ensemble, lat_rows, cell_width), 'member',...  12.3 us
    ppermute x2, starting transfers between devices, padded(): lax.ppermute(tail, axis, [(i, (i + 1) % count) for i in range(ends)])  10.1 us
    all_to_all x1, waiting for transfers between devices, on_device(): lax.all_to_all(jnp.stack(jnp.split(predict_members, lax.axis_size('member...  9.52 us
    all_gather x1, blocking collectives, on_device(): lax.all_gather(innov_here, 'member', axis=0, tiled=True)  8.85 us
    all_gather x1, blocking collectives, on_device(): lax.all_gather(gram_here, 'member', axis=0, tiled=True)  8.35 us
    unnamed x25, local copies, waits for them, and re-layouts  6.76 us
    all_to_all x1, starting transfers between devices, on_device(): lax.all_to_all(sums.reshape(slab_count, lat_rows, tiles_here, 2, PROF), '...  4.3 us
    all_to_all x1, starting transfers between devices, on_device(): lax.all_to_all(jnp.stack(jnp.split(predict_members, lax.axis_size('member...  3.85 us
  transfers between devices with their start and end apart: 6, of which 3 were waited for; matrix products, arithmetic and copies ran while one was open for 10% of the time, Pallas kernels for 0%

profile of v1, /device:TPU:0, one launch (start us, length us, event | category | flops | bytes accessed | tf_op | source)
XLA Modules:
  0.0 82.2 jit_solution(8541940640679141179)
XLA Ops:
  0.0 1.1 %fusion.56 = (f32[2,1,4096]{2,1,0:T(1,128)S(1)}, f32[2,1,4096]{2,1,0:T(1,128)S(1)}) fusion(f32[2,16,4096]{2,1,0:T(8,128)} %param.10), kind=kLoop, calls=%fused_computation.101 | loop fusion | bytes 131072 | tf_op jit(solution)/shard_map/slice | solution.py:18
  1.1 1.3 %collective-permute-start = (f32[2,1,4096]{2,1,0:T(1,128)S(1)}, f32[2,1,4096]{2,1,0:T(1,128)S(1)}, u32[]{:S(2)}, u32[]{:S(2)}) collective-permute-start(f32[2,1,4096]{2,1,0:T(1,128)S(1)} %get-tuple-element.18), channel_id=1, source_target_pairs={{8,0},{16,8},{24,16},{9,1},{17,9},{25,17},{10,2},{18,10},{26,18},{... | collective-permute-start | bytes 98312 | tf_op jit(solution)/shard_map/ppermute | solution.py:23
  2.4 5.6 %collective-permute-start.1 = (f32[2,1,4096]{2,1,0:T(1,128)S(1)}, f32[2,1,4096]{2,1,0:T(1,128)S(1)}, u32[]{:S(2)}, u32[]{:S(2)}) collective-permute-start(f32[2,1,4096]{2,1,0:T(1,128)S(1)} %get-tuple-element.17), channel_id=1, source_target_pairs={{0,8},{8,16},{16,24},{1,9},{9,17},{17,25},{2,10},{10,18},{18,26},{... | collective-permute-start | bytes 98312 | tf_op jit(solution)/shard_map/ppermute | solution.py:21
  8.7 0.6 copy-done.6
  9.3 0.0 copy-done.7
  9.4 0.3 fusion.14
  9.7 0.8 reshape.57
  10.5 4.3 %all-to-all-start.1 = ((f32[4,16,4,2,128]{4,3,2,1,0:T(2,128)}), f32[4,16,4,2,128]{4,3,2,1,0:T(2,128)S(1)}, u32[]{:S(2)}, u32[]{:S(2)}) async-start(f32[4,16,4,2,128]{4,3,2,1,0:T(2,128)} %reshape.57), calls=%async_computation.1 | async-start | bytes 524288 | tf_op jit(solution)/shard_map/all_to_all | solution.py:103
  14.8 0.2 fusion.54
  15.0 0.1 fusion.55
  15.1 0.8 copy-done.2
  15.9 0.9 %copy-done.1 = f32[16,4096]{1,0:T(8,128)S(1)} copy-done((f32[16,4096]{1,0:T(8,128)S(1)}, f32[16,4096]{1,0:T(8,128)}, u32[]{:S(2)}) %copy-start.1) | copy-done | bytes 262168
  16.8 0.4 multiply_add_fusion.1
  17.2 0.2 fusion.51
  17.5 1.3 %collective-permute-start.2 = (f32[2,1,4096]{2,1,0:T(1,128)S(1)}, f32[2,1,4096]{2,1,0:T(1,128)S(1)}, u32[]{:S(2)}, u32[]{:S(2)}) collective-permute-start(f32[2,1,4096]{2,1,0:T(1,128)S(1)} %get-tuple-element.10), channel_id=1, source_target_pairs={{8,0},{16,8},{24,16},{9,1},{17,9},{25,17},{10,2},{18,10},{26,18},{... | collective-permute-start | bytes 98312 | tf_op jit(solution)/shard_map/ppermute | solution.py:23
  18.8 4.6 %collective-permute-start.3 = (f32[2,1,4096]{2,1,0:T(1,128)S(1)}, f32[2,1,4096]{2,1,0:T(1,128)S(1)}, u32[]{:S(2)}, u32[]{:S(2)}) collective-permute-start(f32[2,1,4096]{2,1,0:T(1,128)S(1)} %get-tuple-element.9), channel_id=1, source_target_pairs={{0,8},{8,16},{16,24},{1,9},{9,17},{17,25},{2,10},{10,18},{18,26},{... | collective-permute-start | bytes 98312 | tf_op jit(solution)/shard_map/ppermute | solution.py:21
  23.3 0.1 fusion.52
  23.4 0.1 collective-permute-done.2
  23.5 1.4 %collective-permute-done.3 = f32[2,1,4096]{2,1,0:T(1,128)S(1)} collective-permute-done((f32[2,1,4096]{2,1,0:T(1,128)S(1)}, f32[2,1,4096]{2,1,0:T(1,128)S(1)}, u32[]{:S(2)}, u32[]{:S(2)}) %collective-permute-start.3) | collective-permute-done | bytes 32800 | tf_op jit(solution)/shard_map/ppermute | solution.py:21
  24.9 0.4 multiply_add_fusion
  25.4 0.6 fusion.25
  26.0 0.6 fusion.24
  26.6 0.6 fusion.23
  27.3 0.6 fusion.22
  27.9 0.6 fusion.21
  28.5 0.6 fusion.20
  29.2 0.6 fusion.19
  29.8 0.6 fusion.18
  30.4 3.9 %all-to-all-start = ((f32[8,2,16,512]{3,2,1,0:T(8,128)}), f32[8,2,16,512]{3,2,1,0:T(8,128)S(1)}, u32[]{:S(2)}, u32[]{:S(2)}) async-start(f32[8,2,16,512]{3,2,1,0:T(8,128)} %fusion.18), calls=%async_computation | async-start | bytes 1048576 | tf_op jit(solution)/shard_map/all_to_all | solution.py:74
  34.3 0.1 reduce_sum.28
  34.4 0.1 fusion.57
  34.5 9.5 %all-to-all-done = f32[8,2,16,512]{3,2,1,0:T(8,128)S(1)} async-done(((f32[8,2,16,512]{3,2,1,0:T(8,128)}), f32[8,2,16,512]{3,2,1,0:T(8,128)S(1)}, u32[]{:S(2)}, u32[]{:S(2)}) %all-to-all-start) | async-done | bytes 524320 | tf_op jit(solution)/shard_map/all_to_all | solution.py:74
  44.1 0.2 reshape.56
  44.3 1.1 %convolution_bitcast_fusion.1 = f32[4,16,16]{2,1,0:T(8,128)S(1)} fusion(f32[16,16,4,128]{3,2,1,0:T(4,128)S(1)} %reshape.56, f32[16,4,128]{2,0,1:T(8,128)S(1)} %copy.33, f32[16,4,128]{2,0,1:T(8,128)S(1)} %bitcast.134), kind=kOutput, calls=%fused_computation.16 | convolution fusion | flops 25559040 | bytes 593920 | tf_op jit(solution)/shard_map/irth,jrth->tij/dot_general | solution.py:114
  45.4 8.4 %all_gather.6 = f32[32,16,16]{2,1,0:T(8,128)S(1)} all-gather(f32[4,16,16]{2,1,0:T(8,128)S(1)} %convolution_bitcast_fusion.1), channel_id=1, replica_groups=mesh['slab'=4,'member'=8] {'member'}, dimensions={0}, use_global_device_ids=true | all-gather | bytes 36864 | tf_op jit(solution)/shard_map/all_gather | solution.py:126
  53.8 0.4 multiply_reduce_fusion
  54.2 0.1 broadcast_divide_fusion
  54.3 0.2 fusion.6
  54.5 0.2 fusion.31
  54.6 0.2 fusion.36
  54.8 0.2 fusion.5
  55.0 0.2 fusion.59
  55.2 0.2 fusion.58
  55.3 0.2 fusion.4
  55.5 0.2 fusion.61
  55.7 0.2 fusion.60
  55.8 0.2 fusion.3
  56.0 0.2 fusion.63
  56.2 0.2 fusion.62
  56.3 0.2 fusion.2
  56.5 0.2 fusion.65
  56.7 0.2 fusion.64
  56.9 1.0 %fusion.8 = f32[4,1,16,1]{2,1,3,0:T(1,128)S(1)} fusion(f32[16,16,4,128]{3,2,1,0:T(4,128)S(1)} %reshape.56, f32[16,4,128]{2,0,1:T(8,128)S(1)} %bitcast.135, f32[16,4,128,1]{2,1,0,3:T(4,128)S(1)} %subtract_bitcast_fusion), kind=kOutput, calls=%fused_computation.30 | convolution fusion | flops 1703936 | bytes 590080 | tf_op jit(solution)/shard_map/irth,rth->ti/dot_general | solution.py:117
  57.9 8.9 %all-gather = f32[8,4,16]{2,1,0:T(4,128)S(1)} all-gather(f32[1,4,16]{2,1,0:T(4,128)S(1)} %bitcast.142), channel_id=1, replica_groups=mesh['slab'=4,'member'=8] {'member'}, dimensions={0}, use_global_device_ids=true | all-gather | bytes 2304 | tf_op jit(solution)/shard_map/all_gather | solution.py:132
  66.8 0.1 fusion.43
  66.9 0.2 fusion.1
  67.1 0.2 convolution_divide_fusion
  67.3 0.2 convolution_bitcast_fusion.2
  67.4 0.2 fusion.66
  67.6 0.9 %fusion = f32[16,16,4,128]{3,0,1,2:T(8,128)S(1)} fusion(f32[16,16,4,128]{3,2,1,0:T(4,128)S(1)} %reshape.56, f32[16,4,128]{2,0,1:T(8,128)S(1)} %bitcast.136, f32[4,16,16]{2,1,0:T(8,128)S(1)} %convolution_divide_fusion, f32[4,16]{1,0:T(4,128)S(1)} %bitcast.141), kind=kOutput, calls=%fused_computation.1 | convolution fusion | flops 25430016 | bytes 1085696 | tf_op jit(solution)/shard_map/irth,tij->jrth/dot_general | solution.py:136
  68.5 0.3 copy.38
  68.9 0.2 reshape.58
  69.1 12.3 %all_to_all.28 = f32[16,16,512]{2,1,0:T(8,128)S(1)} all-to-all(f32[16,16,512]{2,1,0:T(8,128)S(1)} %reshape.58), channel_id=1, replica_groups=mesh['slab'=4,'member'=8] {'member'}, dimensions={0} | all-to-all | bytes 1048576 | tf_op jit(solution)/shard_map/all_to_all | solution.py:138
  81.4 0.8 %copy.52 = f32[8,2,2,8,512]{4,3,0,2,1:T(8,128)} copy(f32[8,2,2,8,512]{4,3,2,1,0:T(8,128)S(1)} %bitcast.133) | data formatting | bytes 1048576 | tf_op jit(solution)/shard_map/all_to_all | solution.py:138
  (32 shorter events, 0.3 us)
Async XLA Ops:
  0.0 8.6 %copy-start.4 = (f32[128,128]{1,0:T(8,128)S(1)}, f32[128,128]{1,0:T(8,128)}, u32[]{:S(2)}) copy-start(f32[128,128]{1,0:T(8,128)} %param.13) | copy-start | bytes 196612
  0.0 8.6 %copy-start.3 = (f32[128,128]{1,0:T(8,128)S(1)}, f32[128,128]{1,0:T(8,128)}, u32[]{:S(2)}) copy-start(f32[128,128]{1,0:T(8,128)} %param.14) | copy-start | bytes 196612
  1.1 14.8 %collective-permute-start = (f32[2,1,4096]{2,1,0:T(1,128)S(1)}, f32[2,1,4096]{2,1,0:T(1,128)S(1)}, u32[]{:S(2)}, u32[]{:S(2)}) collective-permute-start(f32[2,1,4096]{2,1,0:T(1,128)S(1)} %get-tuple-element.18), channel_id=1, source_target_pairs={{8,0},{16,8},{24,16},{9,1},{17,9},{25,17},{10,2},{18,10},{26,18},{... | collective-permute-start | bytes 98312 | tf_op jit(solution)/shard_map/ppermute | solution.py:23
  2.4 13.5 %collective-permute-start.1 = (f32[2,1,4096]{2,1,0:T(1,128)S(1)}, f32[2,1,4096]{2,1,0:T(1,128)S(1)}, u32[]{:S(2)}, u32[]{:S(2)}) collective-permute-start(f32[2,1,4096]{2,1,0:T(1,128)S(1)} %get-tuple-element.17), channel_id=1, source_target_pairs={{0,8},{8,16},{16,24},{1,9},{9,17},{17,25},{2,10},{10,18},{18,26},{... | collective-permute-start | bytes 98312 | tf_op jit(solution)/shard_map/ppermute | solution.py:21
  8.7 0.7 copy-start.6
  8.7 0.7 copy-start.7
  8.7 0.7 copy-start.8
  9.6 5.1 %copy-start = (f32[2,16,4096]{2,1,0:T(8,128)S(1)}, f32[2,16,4096]{2,1,0:T(8,128)}, u32[]{:S(2)}) copy-start(f32[2,16,4096]{2,1,0:T(8,128)} %param.10) | copy-start | bytes 1572868
  10.5 20.0 %all-to-all-start.1 = ((f32[4,16,4,2,128]{4,3,2,1,0:T(2,128)}), f32[4,16,4,2,128]{4,3,2,1,0:T(2,128)S(1)}, u32[]{:S(2)}, u32[]{:S(2)}) async-start(f32[4,16,4,2,128]{4,3,2,1,0:T(2,128)} %reshape.57), calls=%async_computation.1 | async-start | bytes 524288 | tf_op jit(solution)/shard_map/all_to_all | solution.py:103
  14.8 1.0 %copy-start.2 = (f32[2,16,4096]{2,1,0:T(8,128)S(1)}, f32[2,16,4096]{2,1,0:T(8,128)}, u32[]{:S(2)}) copy-start(f32[2,16,4096]{2,1,0:T(8,128)} %param.11) | copy-start | bytes 1572868
  15.8 0.9 %copy-start.1 = (f32[16,4096]{1,0:T(8,128)S(1)}, f32[16,4096]{1,0:T(8,128)}, u32[]{:S(2)}) copy-start(f32[16,4096]{1,0:T(8,128)} %param.12) | copy-start | bytes 786436
  17.5 6.0 %collective-permute-start.2 = (f32[2,1,4096]{2,1,0:T(1,128)S(1)}, f32[2,1,4096]{2,1,0:T(1,128)S(1)}, u32[]{:S(2)}, u32[]{:S(2)}) collective-permute-start(f32[2,1,4096]{2,1,0:T(1,128)S(1)} %get-tuple-element.10), channel_id=1, source_target_pairs={{8,0},{16,8},{24,16},{9,1},{17,9},{25,17},{10,2},{18,10},{26,18},{... | collective-permute-start | bytes 98312 | tf_op jit(solution)/shard_map/ppermute | solution.py:23
  18.8 6.1 %collective-permute-start.3 = (f32[2,1,4096]{2,1,0:T(1,128)S(1)}, f32[2,1,4096]{2,1,0:T(1,128)S(1)}, u32[]{:S(2)}, u32[]{:S(2)}) collective-permute-start(f32[2,1,4096]{2,1,0:T(1,128)S(1)} %get-tuple-element.9), channel_id=1, source_target_pairs={{0,8},{8,16},{16,24},{1,9},{9,17},{17,25},{2,10},{10,18},{18,26},{... | collective-permute-start | bytes 98312 | tf_op jit(solution)/shard_map/ppermute | solution.py:21
  30.4 3.9 %copy-start.5 = (s32[1,32,32]{2,1,0:T(8,128)S(1)}, s32[1,32,32]{2,1,0:T(8,128)}, u32[]{:S(2)}) copy-start(s32[1,32,32]{2,1,0:T(8,128)} %param.19) | copy-start | bytes 12292
  30.4 13.6 %all-to-all-start = ((f32[8,2,16,512]{3,2,1,0:T(8,128)}), f32[8,2,16,512]{3,2,1,0:T(8,128)S(1)}, u32[]{:S(2)}, u32[]{:S(2)}) async-start(f32[8,2,16,512]{3,2,1,0:T(8,128)} %fusion.18), calls=%async_computation | async-start | bytes 1048576 | tf_op jit(solution)/shard_map/all_to_all | solution.py:74
